TPU v7x, 256 devices: a whole 4x4x8 slice. The times are simulated.
256 devices in a mesh: cfg: 2 (over y_hi), pipe: 8 (over z), seq: 16 (over x, y_lo, core).
Axes of the slice: x: 4, y: 4 (y_hi: 2, y_lo: 2; y = y_hi * 2 + y_lo), z: 8, core: 2. Of those that a mesh axis runs over, the one named last changes fastest.
Arguments:
- hidden: bfloat16 [2, 512, 4096], P('cfg', 'seq'), may hold values from -6 to 6
- modulation: float32 [8, 3, 4096], P('pipe'), may hold values from -24 to 24
- qkv_weight: bfloat16 [8, 3, 4096, 4096], P('pipe', None, None, 'seq'), may hold values from -4 to 4
- stale_cache: bfloat16 [2, 8, 2, 512, 4096], P('cfg', 'pipe', None, None, 'seq'), may hold values from -6 to 6
- patch_of: int32 [512], P('seq'), may hold values from 0 to 3, as said below
Outputs:
- guided: bfloat16 [512, 4096], P('seq', ('cfg', 'pipe'))
Inputs may be any that keep to these rules, and one draw needn't show every extreme that they name: `patch_of`: each index of seq holds exactly 8 tokens of every patch.
All inputs are finite; a program needn't handle non-finite values.
Results may differ from a plain program's by a relative error of at most 0.035.
Values may be sent and summed in bfloat16 or wider, within the bound.
A program may use at most 64 MiB of HBM per device.

v0:
```python
import jax
import jax.numpy as jnp
from jax import lax
from jax.sharding import PartitionSpec as P

HD = 128
MICRO = 4


GUIDANCE = 5.0
NORM_EPS = 1e-06


def from_behind(block, axis, distance):
    devices = range(lax.axis_size(axis))
    route = [(i - distance, i) for i in devices if i - distance in devices]
    return lax.ppermute(block, axis, route)


def from_root(shard, axis, root):
    mine = lax.axis_index(axis) == root
    return lax.psum(jnp.where(mine, shard, jnp.zeros_like(shard)), axis)


def from_partner(shard, axis, apart):
    return lax.ppermute(shard, axis, [(i, i ^ 1 << apart) for i in range(lax.axis_size(axis))])


def norm_rows(x_float, shift, scale):
    row_mean = jnp.mean(x_float, axis=-1, keepdims=True)
    row_var = jnp.mean(x_float * x_float, axis=-1, keepdims=True) - row_mean * row_mean
    return (x_float - row_mean) * lax.rsqrt(row_var + NORM_EPS) * (1.0 + scale) + shift


def attention(query_rows, key_rows, value_rows):
    head_cols = query_rows.shape[1]
    local_heads = head_cols // HD
    query_heads = query_rows.reshape(query_rows.shape[0], local_heads, HD)
    key_heads = key_rows.reshape(key_rows.shape[0], local_heads, HD)
    value_heads = value_rows.reshape(value_rows.shape[0], local_heads, HD)
    scores = jnp.einsum("phd,thd->hpt", query_heads, key_heads, preferred_element_type=jnp.float32)
    scores = scores * (1.0 / jnp.sqrt(jnp.float32(HD)))
    weights = jax.nn.softmax(scores, axis=-1).astype(jnp.bfloat16)
    output_rows = jnp.einsum(
        "hpt,thd->phd", weights, value_heads, preferred_element_type=jnp.float32
    )
    return output_rows.reshape(query_rows.shape[0], head_cols).astype(jnp.bfloat16)


def attend_patch(query_rows, fresh_kv, kv_buffer, slot_index, is_valid):
    current_kv = lax.dynamic_index_in_dim(kv_buffer, slot_index, 1, keepdims=False)
    kept_kv = jnp.where(is_valid, fresh_kv, current_kv)
    kv_buffer = lax.dynamic_update_index_in_dim(kv_buffer, kept_kv, slot_index, 1)
    head_cols = kv_buffer.shape[-1]
    key_rows = kv_buffer[0].reshape(-1, head_cols)
    value_rows = kv_buffer[1].reshape(-1, head_cols)
    return (attention(query_rows, key_rows, value_rows), kv_buffer)


def body(hidden, modulation, qkv_weight, stale_cache, patch_of):
    pipe_rank = lax.axis_index("pipe")
    branch_rank = lax.axis_index("cfg")
    seq_count = lax.axis_size("seq")
    pipe_count = lax.axis_size("pipe")
    x_local = hidden[0]
    gains_all = modulation[0]
    weights_local = qkv_weight[0]
    tok_dev, model_width = x_local.shape
    row_count = tok_dev // MICRO
    head_cols = stale_cache.shape[-1]
    group_rows = seq_count * row_count
    tick_count = MICRO + pipe_count - 1
    row_order = jnp.argsort(patch_of, stable=True)
    x_sorted = x_local[row_order]
    every_order = lax.all_gather(row_order, "seq", axis=0, tiled=True)
    offsets = (jnp.arange(seq_count, dtype=jnp.int32) * tok_dev)[:, None, None]
    positions = (
        (every_order.reshape(seq_count, MICRO, row_count) + offsets).transpose(1, 0, 2).reshape(-1)
    )
    stale_rows = stale_cache[0, 0][:, positions, :].reshape(2, MICRO, group_rows, head_cols)

    def patch_slot(tick):
        offset_tick = tick - pipe_rank
        is_valid = jnp.logical_and(offset_tick >= 0, offset_tick < MICRO)
        return (jnp.clip(offset_tick, 0, MICRO - 1), is_valid)

    def project(piece):
        return jnp.einsum(
            "rd,cdh->crh", piece, weights_local, preferred_element_type=jnp.float32
        ).astype(jnp.bfloat16)

    def advance(tick, carry):
        incoming, kv_buffer, results = carry
        slot_index, is_valid = patch_slot(tick)
        own_rows = lax.dynamic_slice_in_dim(x_sorted, slot_index * row_count, row_count, 0)
        layer_in = jnp.where(pipe_rank == 0, own_rows, incoming)
        x_float = layer_in.astype(jnp.float32)
        normed = norm_rows(x_float, gains_all[0], gains_all[1]).astype(jnp.bfloat16)
        projected = project(lax.all_gather(normed, "seq", axis=0, tiled=True))
        mixed_rows, kv_buffer = attend_patch(
            projected[0], projected[1:], kv_buffer, slot_index, is_valid
        )
        back_rows = lax.all_to_all(mixed_rows, "seq", split_axis=0, concat_axis=1, tiled=True)
        updated = (x_float + gains_all[2] * back_rows.astype(jnp.float32)).astype(jnp.bfloat16)
        old_rows = lax.dynamic_slice_in_dim(results, slot_index * row_count, row_count, 0)
        results = lax.dynamic_update_slice_in_dim(
            results, jnp.where(is_valid, updated, old_rows), slot_index * row_count, 0
        )
        incoming = from_behind(updated, "pipe", 1)
        return (incoming, kv_buffer, results)

    initial = (
        jnp.zeros((row_count, model_width), jnp.bfloat16),
        stale_rows,
        jnp.zeros((tok_dev, model_width), jnp.bfloat16),
    )
    final_sorted = lax.fori_loop(0, tick_count, advance, initial)[2]
    inverse = jnp.argsort(row_order)
    final_rows = final_sorted[inverse]
    whole_rows = from_root(final_rows, "pipe", pipe_count - 1)
    col_count = model_width // (2 * pipe_count)
    own_start = (branch_rank * pipe_count + pipe_rank) * col_count
    partner_start = ((1 - branch_rank) * pipe_count + pipe_rank) * col_count
    own_cols = lax.dynamic_slice_in_dim(whole_rows, own_start, col_count, 1)
    partner_cols = lax.dynamic_slice_in_dim(whole_rows, partner_start, col_count, 1)
    other_cols = from_partner(partner_cols, "cfg", 0)
    cond_pred = jnp.where(branch_rank == 0, own_cols, other_cols).astype(jnp.float32)
    uncond_pred = jnp.where(branch_rank == 0, other_cols, own_cols).astype(jnp.float32)
    return (uncond_pred + GUIDANCE * (cond_pred - uncond_pred)).astype(jnp.bfloat16)


def solution(mesh):
    placed = (
        P("cfg", "seq", None),
        P("pipe", None, None),
        P("pipe", None, None, "seq"),
        P("cfg", "pipe", None, None, "seq"),
        P("seq"),
    )
    return jax.shard_map(
        body, mesh=mesh, in_specs=placed, out_specs=P("seq", ("cfg", "pipe")), check_vma=False
    )
```

profile of v0, /device:TPU:1, one launch (start us, length us, event | category | flops | bytes accessed | tf_op | source)
XLA Modules:
  0.0 780.4 jit_solution(249356345029768014)
XLA Ops:
  13.6 10.8 %all-reduce = s32[512]{0:T(512)S(1)} all-reduce(s32[512]{0:T(512)S(1)} %dynamic-update-slice), channel_id=1, replica_groups=mesh['cfg'=2,'pipe'=8,'seq'=16] {'seq'}, use_global_device_ids=true, to_apply=%add | all-reduce | flops 512 | bytes 4096
  30.8 664.2 %while.18 = (s32[]{:T(128)}, bf16[8,4096]{1,0:T(8,128)(2,1)S(1)}, bf16[2,4,128,256]{3,2,1,0:T(8,128)(2,1)S(1)}, bf16[32,4096]{1,0:T(8,128)(2,1)S(1)}, pred[]{:T(...) while((s32[]{:T(128)}, bf16[8,4096]{1,0:T(8,128)(2,1)S(1)}, ...), condition=%wide.region_6.7_spmd, body=%wide.region_1.6_spmd.sunk | while | flops 907646272 | bytes 17648212 | solution.py:117
  31.9 40.0 %all-gather.2.cloned.1.call-done = bf16[128,4096]{1,0:T(8,128)(2,1)} async-done(((bf16[8,4096]{1,0:T(8,128)(2,1)}), bf16[128,4096]{1,0:T(8,128)(2,1)}) %all-gather.2.cloned.1.call-update) | async-done | bytes 1048592 | tf_op jit(solution)/shard_map/while/body/eval_jaxpr/all_gather | solution.py:99
  77.8 9.9 %all_to_all.28 = bf16[16,8,256]{2,1,0:T(8,128)(2,1)S(1)} all-to-all(bf16[16,8,256]{2,1,0:T(8,128)(2,1)S(1)} %convert_element_type.138), channel_id=1, replica_groups=mesh['cfg'=2,'pipe'=8,'seq'=16] {'seq'}, dimensions={0} | all-to-all | bytes 131072 | tf_op jit(solution)/shard_map/while/body/eval_jaxpr/all_to_all | solution.py:103
  93.3 39.0 %all-gather.2.cloned.1.call-done = bf16[128,4096]{1,0:T(8,128)(2,1)} async-done(((bf16[8,4096]{1,0:T(8,128)(2,1)}), bf16[128,4096]{1,0:T(8,128)(2,1)}) %all-gather.2.cloned.1.call-update) | async-done | bytes 1048592 | tf_op jit(solution)/shard_map/while/body/eval_jaxpr/all_gather | solution.py:99
  138.2 9.9 %all_to_all.28 = bf16[16,8,256]{2,1,0:T(8,128)(2,1)S(1)} all-to-all(bf16[16,8,256]{2,1,0:T(8,128)(2,1)S(1)} %convert_element_type.138), channel_id=1, replica_groups=mesh['cfg'=2,'pipe'=8,'seq'=16] {'seq'}, dimensions={0} | all-to-all | bytes 131072 | tf_op jit(solution)/shard_map/while/body/eval_jaxpr/all_to_all | solution.py:103
  153.7 39.0 %all-gather.2.cloned.1.call-done = bf16[128,4096]{1,0:T(8,128)(2,1)} async-done(((bf16[8,4096]{1,0:T(8,128)(2,1)}), bf16[128,4096]{1,0:T(8,128)(2,1)}) %all-gather.2.cloned.1.call-update) | async-done | bytes 1048592 | tf_op jit(solution)/shard_map/while/body/eval_jaxpr/all_gather | solution.py:99
  198.6 9.9 %all_to_all.28 = bf16[16,8,256]{2,1,0:T(8,128)(2,1)S(1)} all-to-all(bf16[16,8,256]{2,1,0:T(8,128)(2,1)S(1)} %convert_element_type.138), channel_id=1, replica_groups=mesh['cfg'=2,'pipe'=8,'seq'=16] {'seq'}, dimensions={0} | all-to-all | bytes 131072 | tf_op jit(solution)/shard_map/while/body/eval_jaxpr/all_to_all | solution.py:103
  214.1 38.7 %all-gather.2.cloned.1.call-done = bf16[128,4096]{1,0:T(8,128)(2,1)} async-done(((bf16[8,4096]{1,0:T(8,128)(2,1)}), bf16[128,4096]{1,0:T(8,128)(2,1)}) %all-gather.2.cloned.1.call-update) | async-done | bytes 1048592 | tf_op jit(solution)/shard_map/while/body/eval_jaxpr/all_gather | solution.py:99
  258.6 9.9 %all_to_all.28 = bf16[16,8,256]{2,1,0:T(8,128)(2,1)S(1)} all-to-all(bf16[16,8,256]{2,1,0:T(8,128)(2,1)S(1)} %convert_element_type.138), channel_id=1, replica_groups=mesh['cfg'=2,'pipe'=8,'seq'=16] {'seq'}, dimensions={0} | all-to-all | bytes 131072 | tf_op jit(solution)/shard_map/while/body/eval_jaxpr/all_to_all | solution.py:103
  274.1 38.7 %all-gather.2.cloned.1.call-done = bf16[128,4096]{1,0:T(8,128)(2,1)} async-done(((bf16[8,4096]{1,0:T(8,128)(2,1)}), bf16[128,4096]{1,0:T(8,128)(2,1)}) %all-gather.2.cloned.1.call-update) | async-done | bytes 1048592 | tf_op jit(solution)/shard_map/while/body/eval_jaxpr/all_gather | solution.py:99
  318.7 9.9 %all_to_all.28 = bf16[16,8,256]{2,1,0:T(8,128)(2,1)S(1)} all-to-all(bf16[16,8,256]{2,1,0:T(8,128)(2,1)S(1)} %convert_element_type.138), channel_id=1, replica_groups=mesh['cfg'=2,'pipe'=8,'seq'=16] {'seq'}, dimensions={0} | all-to-all | bytes 131072 | tf_op jit(solution)/shard_map/while/body/eval_jaxpr/all_to_all | solution.py:103
  334.2 38.7 %all-gather.2.cloned.1.call-done = bf16[128,4096]{1,0:T(8,128)(2,1)} async-done(((bf16[8,4096]{1,0:T(8,128)(2,1)}), bf16[128,4096]{1,0:T(8,128)(2,1)}) %all-gather.2.cloned.1.call-update) | async-done | bytes 1048592 | tf_op jit(solution)/shard_map/while/body/eval_jaxpr/all_gather | solution.py:99
  378.8 9.9 %all_to_all.28 = bf16[16,8,256]{2,1,0:T(8,128)(2,1)S(1)} all-to-all(bf16[16,8,256]{2,1,0:T(8,128)(2,1)S(1)} %convert_element_type.138), channel_id=1, replica_groups=mesh['cfg'=2,'pipe'=8,'seq'=16] {'seq'}, dimensions={0} | all-to-all | bytes 131072 | tf_op jit(solution)/shard_map/while/body/eval_jaxpr/all_to_all | solution.py:103
  394.3 39.0 %all-gather.2.cloned.1.call-done = bf16[128,4096]{1,0:T(8,128)(2,1)} async-done(((bf16[8,4096]{1,0:T(8,128)(2,1)}), bf16[128,4096]{1,0:T(8,128)(2,1)}) %all-gather.2.cloned.1.call-update) | async-done | bytes 1048592 | tf_op jit(solution)/shard_map/while/body/eval_jaxpr/all_gather | solution.py:99
  439.2 9.9 %all_to_all.28 = bf16[16,8,256]{2,1,0:T(8,128)(2,1)S(1)} all-to-all(bf16[16,8,256]{2,1,0:T(8,128)(2,1)S(1)} %convert_element_type.138), channel_id=1, replica_groups=mesh['cfg'=2,'pipe'=8,'seq'=16] {'seq'}, dimensions={0} | all-to-all | bytes 131072 | tf_op jit(solution)/shard_map/while/body/eval_jaxpr/all_to_all | solution.py:103
  454.7 39.0 %all-gather.2.cloned.1.call-done = bf16[128,4096]{1,0:T(8,128)(2,1)} async-done(((bf16[8,4096]{1,0:T(8,128)(2,1)}), bf16[128,4096]{1,0:T(8,128)(2,1)}) %all-gather.2.cloned.1.call-update) | async-done | bytes 1048592 | tf_op jit(solution)/shard_map/while/body/eval_jaxpr/all_gather | solution.py:99
  499.6 9.9 %all_to_all.28 = bf16[16,8,256]{2,1,0:T(8,128)(2,1)S(1)} all-to-all(bf16[16,8,256]{2,1,0:T(8,128)(2,1)S(1)} %convert_element_type.138), channel_id=1, replica_groups=mesh['cfg'=2,'pipe'=8,'seq'=16] {'seq'}, dimensions={0} | all-to-all | bytes 131072 | tf_op jit(solution)/shard_map/while/body/eval_jaxpr/all_to_all | solution.py:103
  515.1 39.0 %all-gather.2.cloned.1.call-done = bf16[128,4096]{1,0:T(8,128)(2,1)} async-done(((bf16[8,4096]{1,0:T(8,128)(2,1)}), bf16[128,4096]{1,0:T(8,128)(2,1)}) %all-gather.2.cloned.1.call-update) | async-done | bytes 1048592 | tf_op jit(solution)/shard_map/while/body/eval_jaxpr/all_gather | solution.py:99
  575.5 38.7 %all-gather.2.cloned.1.call-done = bf16[128,4096]{1,0:T(8,128)(2,1)} async-done(((bf16[8,4096]{1,0:T(8,128)(2,1)}), bf16[128,4096]{1,0:T(8,128)(2,1)}) %all-gather.2.cloned.1.call-update) | async-done | bytes 1048592 | tf_op jit(solution)/shard_map/while/body/eval_jaxpr/all_gather | solution.py:99
  620.1 9.9 %all_to_all.28 = bf16[16,8,256]{2,1,0:T(8,128)(2,1)S(1)} all-to-all(bf16[16,8,256]{2,1,0:T(8,128)(2,1)S(1)} %convert_element_type.138), channel_id=1, replica_groups=mesh['cfg'=2,'pipe'=8,'seq'=16] {'seq'}, dimensions={0} | all-to-all | bytes 131072 | tf_op jit(solution)/shard_map/while/body/eval_jaxpr/all_to_all | solution.py:103
  635.6 39.0 %all-gather.2.cloned.1.call-done = bf16[128,4096]{1,0:T(8,128)(2,1)} async-done(((bf16[8,4096]{1,0:T(8,128)(2,1)}), bf16[128,4096]{1,0:T(8,128)(2,1)}) %all-gather.2.cloned.1.call-update) | async-done | bytes 1048592 | tf_op jit(solution)/shard_map/while/body/eval_jaxpr/all_gather | solution.py:99
  680.5 9.9 %all_to_all.28 = bf16[16,8,256]{2,1,0:T(8,128)(2,1)S(1)} all-to-all(bf16[16,8,256]{2,1,0:T(8,128)(2,1)S(1)} %convert_element_type.138), channel_id=1, replica_groups=mesh['cfg'=2,'pipe'=8,'seq'=16] {'seq'}, dimensions={0} | all-to-all | bytes 131072 | tf_op jit(solution)/shard_map/while/body/eval_jaxpr/all_to_all | solution.py:103
  696.4 70.7 %all-reduce.3.cloned.1.call-done = bf16[32,4096]{1,0:T(8,128)(2,1)} async-done(((bf16[32,4096]{1,0:T(8,128)(2,1)}), bf16[32,4096]{1,0:T(8,128)(2,1)}) %all-reduce.3.cloned.1.call-update) | async-done | bytes 262160 | tf_op jit(solution)/shard_map/psum | solution.py:22
  (289 shorter events, 154.1 us)
Async XLA Ops:
  30.8 41.1 %all-gather.2.cloned.1.call-start = ((), (), s32[]{:S(2)}) async-start(), calls=%async_computation.2 | async-start | bytes 1114112 | tf_op jit(solution)/shard_map/while/body/eval_jaxpr/all_gather | solution.py:99
  87.7 4.5 collective-permute-start
  92.2 40.0 %all-gather.2.cloned.1.call-start = ((), (), s32[]{:S(2)}) async-start(), calls=%async_computation.2 | async-start | bytes 1114112 | tf_op jit(solution)/shard_map/while/body/eval_jaxpr/all_gather | solution.py:99
  148.1 4.5 collective-permute-start
  152.6 40.0 %all-gather.2.cloned.1.call-start = ((), (), s32[]{:S(2)}) async-start(), calls=%async_computation.2 | async-start | bytes 1114112 | tf_op jit(solution)/shard_map/while/body/eval_jaxpr/all_gather | solution.py:99
  208.5 4.5 collective-permute-start
  213.0 39.7 %all-gather.2.cloned.1.call-start = ((), (), s32[]{:S(2)}) async-start(), calls=%async_computation.2 | async-start | bytes 1114112 | tf_op jit(solution)/shard_map/while/body/eval_jaxpr/all_gather | solution.py:99
  268.6 4.5 collective-permute-start
  273.1 39.7 %all-gather.2.cloned.1.call-start = ((), (), s32[]{:S(2)}) async-start(), calls=%async_computation.2 | async-start | bytes 1114112 | tf_op jit(solution)/shard_map/while/body/eval_jaxpr/all_gather | solution.py:99
  328.7 4.5 collective-permute-start
  333.2 39.7 %all-gather.2.cloned.1.call-start = ((), (), s32[]{:S(2)}) async-start(), calls=%async_computation.2 | async-start | bytes 1114112 | tf_op jit(solution)/shard_map/while/body/eval_jaxpr/all_gather | solution.py:99
  388.8 4.5 collective-permute-start
  393.3 40.0 %all-gather.2.cloned.1.call-start = ((), (), s32[]{:S(2)}) async-start(), calls=%async_computation.2 | async-start | bytes 1114112 | tf_op jit(solution)/shard_map/while/body/eval_jaxpr/all_gather | solution.py:99
  449.2 4.5 collective-permute-start
  453.7 40.0 %all-gather.2.cloned.1.call-start = ((), (), s32[]{:S(2)}) async-start(), calls=%async_computation.2 | async-start | bytes 1114112 | tf_op jit(solution)/shard_map/while/body/eval_jaxpr/all_gather | solution.py:99
  509.6 4.5 collective-permute-start
  514.1 40.0 %all-gather.2.cloned.1.call-start = ((), (), s32[]{:S(2)}) async-start(), calls=%async_computation.2 | async-start | bytes 1114112 | tf_op jit(solution)/shard_map/while/body/eval_jaxpr/all_gather | solution.py:99
  570.0 4.5 collective-permute-start
  574.5 39.7 %all-gather.2.cloned.1.call-start = ((), (), s32[]{:S(2)}) async-start(), calls=%async_computation.2 | async-start | bytes 1114112 | tf_op jit(solution)/shard_map/while/body/eval_jaxpr/all_gather | solution.py:99
  630.1 4.5 collective-permute-start
  634.6 40.0 %all-gather.2.cloned.1.call-start = ((), (), s32[]{:S(2)}) async-start(), calls=%async_computation.2 | async-start | bytes 1114112 | tf_op jit(solution)/shard_map/while/body/eval_jaxpr/all_gather | solution.py:99
  690.5 4.5 collective-permute-start
  694.9 72.2 %all-reduce.3.cloned.1.call-start = ((), (), s32[]{:S(2)}) async-start(), calls=%async_computation.1 | async-start | bytes 524288 | tf_op jit(solution)/shard_map/psum | solution.py:22
  767.9 4.1 collective-permute-start.1
  (1 other events, 22.6 us)
Sparse Core Ops, SparseCore 0:
  33.6 38.2 all-gather.1
  95.1 37.1 all-gather.1
  155.5 37.1 all-gather.1
  215.5 37.1 all-gather.1
  275.6 37.1 all-gather.1
  335.7 37.1 all-gather.1
  396.1 37.1 all-gather.1
  456.5 37.1 all-gather.1
  516.9 37.1 all-gather.1
  577.0 37.1 all-gather.1
  637.4 37.1 all-gather.1
Sparse Core Ops, SparseCore 1:
  697.7 69.4 all-reduce.2
where the time goes:
time: 787 us; the launch traced here: 780 us
  waiting for transfers between devices  515 us (65%)
  blocking collectives  120 us (15%)
  matrix products  59.4 us (8%)
  starting transfers between devices  37.8 us (5%)
  other arithmetic  17.6 us (2%)
  between operations  15.3 us (2%)
  local copies, waits for them, and re-layouts  13.4 us (2%)
    all_gather x11, waiting for transfers between devices, advance(): projected = project(lax.all_gather(normed, 'seq', axis=0, tiled=True))  429 us
    all_to_all x11, blocking collectives, advance(): lax.all_to_all(mixed_rows, 'seq', split_axis=0, concat_axis=1, tiled=True)  109 us
    psum x1, waiting for transfers between devices, from_root(): return lax.psum(jnp.where(mine, shard, jnp.zeros_like(shard)), axis)  70.7 us
    dot_general x11, matrix products, project(): jnp.einsum('rd,cdh->crh', piece, weights_local, preferred_element_type=jn...  45.1 us
    ppermute x11, starting transfers between devices, from_behind(): return lax.ppermute(block, axis, route)  35 us
  transfers between devices with their start and end apart: 24, of which 24 were waited for; matrix products, arithmetic and copies ran while one was open for 0% of the time, Pallas kernels for 0%

commit v1 on v0

v1 whole, which is shorter than its diff:
```python
import functools

import jax
import jax.numpy as jnp
from jax import lax
from jax.experimental import pallas as pl
from jax.experimental.pallas import tpu as pltpu
from jax.sharding import PartitionSpec as P

F32 = jnp.float32
BF16 = jnp.bfloat16
MESH = pl.DeviceIdType.MESH

HD = 128
D = 4096
MICRO = 4
ROWS = 128
COLS = 256
SEQ = 16
PIPE = 8
GUIDANCE = 5.0
NORM_EPS = 1e-06

DIRECT = ((0, 0), (0, 1), (2, 0), (2, 1))
RELAY = ((1, 0), (3, 0), (1, 1), (3, 1))
OTHERS = DIRECT[1:] + RELAY
N_PLANE = len(OTHERS)
OWN_SIB = N_PLANE
FWD = OWN_SIB + 1
NEXT = FWD + N_PLANE
N_SEND = NEXT + len(DIRECT)
CHUNKS = 2
CW = COLS // CHUNKS


def kernel(
    hid_hbm, mod_hbm, w_hbm, stale_hbm, patch_ref, out_ref,
    x_buf, w_buf, hid, mod, stale, sorted_rows, kv, acc, sum1, sum2, colsum, shifted,
    pos_buf, x_out, fin_out, fin_in,
    load_sem, w_sem, pos_send, pos_recv, send_sem, recv_sem, fin_send, fin_recv,
):
    c = lax.axis_index("cfg")
    s = lax.axis_index("pipe")
    i = lax.axis_index("seq")
    core = i % 2
    y = (i // 2) % 2
    x = i // 4
    is_first = s == 0
    is_last = s == PIPE - 1

    def at(off, other=0):
        return (((x + off[0]) % 4) * 2 + (y + off[1]) % 2) * 2 + (core + other) % 2

    sib = at((0, 0), 1)
    out_col = c * PIPE + s

    loads = [
        pltpu.make_async_copy(hid_hbm.at[0], hid, load_sem.at[0]),
        pltpu.make_async_copy(mod_hbm.at[0], mod, load_sem.at[1]),
        pltpu.make_async_copy(stale_hbm.at[0, 0], stale, load_sem.at[2]),
    ]

    def w_copy(b):
        return pltpu.make_async_copy(
            w_hbm.at[0, :, pl.ds(pl.multiple_of(b * COLS, COLS), COLS), :], w_buf.at[b], w_sem.at[b]
        )

    barrier = pltpu.get_barrier_semaphore()

    def greet(target):
        pl.semaphore_signal(barrier, inc=1, device_id=target, device_id_type=MESH)

    def greet_plane(k, carry):
        greet((c, s, (i + k) % SEQ))
        return carry

    lax.fori_loop(1, SEQ, greet_plane, 0)

    @pl.when(s > 0)
    def _():
        for off in DIRECT:
            greet((c, s - 1, at(off)))

    for branch in range(2):
        is_self = jnp.logical_and(jnp.logical_and(c == branch, is_last), i == out_col)

        @pl.when(jnp.logical_not(is_self))
        def _():
            greet((branch, PIPE - 1, out_col))

    for load in loads:
        load.start()

    def start_w(b, carry):
        w_copy(b).start()
        return carry

    lax.fori_loop(0, SEQ, start_w, 0)

    patch_row = jnp.broadcast_to(patch_ref[...].astype(F32), (32, 32))
    row32 = lax.broadcasted_iota(jnp.int32, (32, 32), 0)
    col32 = lax.broadcasted_iota(jnp.int32, (32, 32), 1)
    patch_col = jnp.sum(jnp.where(row32 == col32, patch_row, 0.0), axis=1, keepdims=True)
    same = jnp.where(patch_row == patch_col, 1.0, 0.0)
    rank_col = jnp.sum(jnp.where(col32 < row32, same, 0.0), axis=1, keepdims=True)
    rank_row = jnp.sum(jnp.where(row32 < col32, same, 0.0), axis=0, keepdims=True)
    pos_row = patch_row[0:1] * 8.0 + rank_row
    pos_col = patch_col * 8.0 + rank_col
    to_sorted = jnp.where(pos_row == row32.astype(F32), 1.0, 0.0).astype(BF16)
    from_sorted = jnp.where(pos_col == col32.astype(F32), 1.0, 0.0).astype(BF16)
    whole_pos = patch_col * float(ROWS) + rank_col + (i * 8).astype(F32)
    row128 = lax.broadcasted_iota(jnp.int32, (32, 128), 0)
    lane128 = lax.broadcasted_iota(jnp.int32, (32, 128), 1)
    placed = jnp.where(lane128 == row128 + (i % 4) * 32, whole_pos, 0.0)
    pos_buf[i] = jnp.broadcast_to(jnp.sum(placed, axis=0, keepdims=True), (8, 128))

    is_own_out = jnp.logical_and(is_last, i == out_col)
    expected = (
        (SEQ - 1)
        + jnp.where(is_last, SEQ, len(DIRECT))
        - jnp.where(is_own_out, 1, 0)
    )
    pl.semaphore_wait(barrier, expected)

    def pos_copy(k):
        return pltpu.make_async_remote_copy(
            src_ref=pos_buf.at[i], dst_ref=pos_buf.at[i], send_sem=pos_send.at[k], recv_sem=pos_recv.at[i],
            device_id=(c, s, (i + k) % SEQ), device_id_type=MESH,
        )

    def pos_arrival(b):
        return pltpu.make_async_remote_copy(
            src_ref=pos_buf.at[b], dst_ref=pos_buf.at[b], send_sem=pos_send.at[0], recv_sem=pos_recv.at[b],
            device_id=(c, s, sib), device_id_type=MESH,
        )

    def slot_of(m):
        return m + jnp.where(is_first, MICRO, 0)

    def block_copy(m, b, k, number, target, slot):
        return pltpu.make_async_remote_copy(
            src_ref=x_buf.at[slot, b, k], dst_ref=x_buf.at[slot, b, k],
            send_sem=send_sem.at[m, number, k], recv_sem=recv_sem.at[m, b, k],
            device_id=(c, s, target), device_id_type=MESH,
        )

    def next_copy(m, k, n):
        return pltpu.make_async_remote_copy(
            src_ref=x_out.at[m, k], dst_ref=x_buf.at[m, i, k],
            send_sem=send_sem.at[m, NEXT + n, k], recv_sem=recv_sem.at[m, i, k],
            device_id=(c, s + 1, at(DIRECT[n])), device_id_type=MESH,
        )

    def arrive(m, b, k):
        block_copy(m, b, k, 0, sib, slot_of(m)).wait_recv()

    def spread_own(m):
        slot = slot_of(m)
        for k in range(CHUNKS):
            @pl.when(s > 0)
            def _():
                arrive(m, i, k)

            for n, off in enumerate(OTHERS):
                if off in RELAY:
                    block_copy(m, i, k, n, at(off), slot).start()
                else:
                    @pl.when(is_first)
                    def _():
                        block_copy(m, i, k, n, at(off), slot).start()

            block_copy(m, i, k, OWN_SIB, sib, slot).start()

    def take(m, number):
        b = at(OTHERS[number])
        for k in range(CHUNKS):
            arrive(m, b, k)
            block_copy(m, b, k, FWD + number, sib, slot_of(m)).start()

    @pl.when(is_first)
    def _():
        loads[0].wait()
        sorted_rows[...] = jnp.dot(to_sorted, hid[...], preferred_element_type=F32)
        for m in range(MICRO):
            for k in range(CHUNKS):
                pieces = [
                    sorted_rows[8 * m : 8 * m + 8, COLS * j + CW * k : COLS * j + CW * (k + 1)] for j in range(SEQ)
                ]
                x_buf[MICRO + m, i, k] = jnp.concatenate(pieces, axis=0).astype(BF16)
            if m == 0:
                spread_own(0)

    @pl.when(s > 0)
    def _():
        loads[0].wait()

    def send_pos(k, carry):
        pos_copy(k).start()
        return carry

    lax.fori_loop(1, SEQ, send_pos, 0)

    loads[1].wait()
    colsum[...] = jnp.zeros_like(colsum)
    shifted[...] = jnp.zeros_like(shifted)

    def fold(b, carry):
        w_copy(b).wait()
        span = pl.ds(pl.multiple_of(b * COLS, COLS), COLS)
        gain = jnp.broadcast_to(1.0 + mod[1:2, span], (128, COLS)).T
        gain = jnp.concatenate([gain, gain], axis=1)
        shift = jnp.broadcast_to(mod[0:1, span], (8, COLS))
        shift_high = shift.astype(BF16)
        shift_low = (shift - shift_high.astype(F32)).astype(BF16)
        shift_both = jnp.concatenate([shift_high, shift_low], axis=0)
        ones = jnp.ones((8, COLS), BF16)
        for t in range(3):
            raw = w_buf[b, t]
            shifted[t] += jnp.dot(shift_both, raw, preferred_element_type=F32)
            scaled = (raw.astype(F32) * gain).astype(BF16)
            w_buf[b, t] = scaled
            colsum[t] += jnp.dot(ones, scaled, preferred_element_type=F32)
        return carry

    lax.fori_loop(0, SEQ, fold, 0)

    loads[2].wait()

    def wait_pos(k, carry):
        pos_arrival((i + k) % SEQ).wait_recv()
        return carry

    lax.fori_loop(1, SEQ, wait_pos, 0)
    pos_all = jnp.concatenate(
        [sum(pos_buf[4 * g + n, 0:1, :] for n in range(4)) for g in range(4)], axis=1
    )
    for g in range(4):
        rows = lax.broadcasted_iota(jnp.int32, (128, 512), 0).astype(F32) + float(128 * g)
        pick = jnp.where(pos_all == rows, 1.0, 0.0).astype(BF16)
        for t in range(2):
            kv[t, 128 * g : 128 * g + 128, :] = jnp.dot(
                pick, stale[t], preferred_element_type=F32
            ).astype(BF16)

    @pl.when(s > 0)
    def _():
        spread_own(0)

    def block(m, b):
        return jnp.concatenate([x_buf[m, b, k] for k in range(CHUNKS)], axis=1)

    def project(m, blocks, fresh):
        parts = [block(m, b) for b in blocks]
        for t in range(3):
            total = sum(
                jnp.dot(part, w_buf[b, t], preferred_element_type=F32) for part, b in zip(parts, blocks)
            )
            acc[t] = total if fresh else acc[t] + total
        one = jnp.zeros((ROWS, 128), F32) if fresh else sum1[...]
        two = jnp.zeros((ROWS, 128), F32) if fresh else sum2[...]
        for part in parts:
            wide = part.astype(F32)
            square = wide * wide
            one = one + wide[:, :128] + wide[:, 128:]
            two = two + square[:, :128] + square[:, 128:]
        sum1[...] = one
        sum2[...] = two

    scaling = 1.0 / (HD ** 0.5)

    def patch_step(m, carry):
        @pl.when(is_first)
        def _():
            for number in range(N_PLANE):
                take(m, number)
            for off in DIRECT + RELAY:
                for k in range(CHUNKS):
                    arrive(m, at(off, 1), k)

            def regroup(jj, inner):
                span = pl.ds(pl.multiple_of(jj * 16, 16), 16)
                for k in range(CHUNKS):
                    pieces = [x_buf[MICRO + m, b, k, span, :].astype(F32) for b in range(SEQ)]
                    for half in range(2):
                        x_buf[m, 2 * jj + half, k] = jnp.concatenate(
                            [piece[8 * half : 8 * half + 8] for piece in pieces], axis=0
                        ).astype(BF16)
                return inner

            lax.fori_loop(0, SEQ // 2, regroup, 0)

        n_direct = len(DIRECT) - 1

        @pl.when(s > 0)
        def _():
            for number in range(n_direct):
                take(m, number)

        project(m, [at(off) for off in DIRECT], True)

        @pl.when(s > 0)
        def _():
            for number in range(n_direct, N_PLANE):
                take(m, number)

        project(m, [at(off) for off in RELAY], False)

        for group in (DIRECT, RELAY):
            @pl.when(s > 0)
            def _():
                for off in group:
                    for k in range(CHUNKS):
                        arrive(m, at(off, 1), k)

            project(m, [at(off, 1) for off in group], False)

        @pl.when(m < MICRO - 1)
        def _():
            spread_own(m + 1)

        mean = jnp.sum(sum1[...], axis=1, keepdims=True) * (1.0 / D)
        var = jnp.sum(sum2[...], axis=1, keepdims=True) * (1.0 / D) - mean * mean
        inv = lax.rsqrt(var + NORM_EPS)

        def finish(t):
            bias = shifted[t, 0:1] + shifted[t, 8:9]
            return (inv * (acc[t] - mean * colsum[t, 0:1]) + bias).astype(BF16)

        query = finish(0)
        rows = pl.ds(pl.multiple_of(m * ROWS, ROWS), ROWS)
        kv[0, rows, :] = finish(1)
        kv[1, rows, :] = finish(2)
        own = pl.ds(pl.multiple_of(i * COLS, COLS), COLS)
        gate = mod[2:3, own]
        old = block(m, i)
        for h in range(2):
            cols = slice(h * HD, (h + 1) * HD)
            scores = lax.dot_general(
                query[:, cols], kv[0, :, cols], (((1,), (1,)), ((), ())), preferred_element_type=F32
            )
            top = jnp.max(scores, axis=1, keepdims=True)
            weights = jnp.exp((scores - top) * scaling)
            norm = jnp.sum(weights, axis=1, keepdims=True)
            mixed = jnp.dot(weights.astype(BF16), kv[1, :, cols], preferred_element_type=F32) / norm
            mixed = mixed.astype(BF16).astype(F32)
            fresh = (old[:, cols].astype(F32) + gate[:, cols] * mixed).astype(BF16)
            if CHUNKS == 2:
                x_out[m, h] = fresh
            else:
                x_out[m, 0, :, cols] = fresh
            if CHUNKS == 2 or h == 1:
                @pl.when(s < PIPE - 1)
                def _():
                    for n in range(len(DIRECT)):
                        next_copy(m, h if CHUNKS == 2 else 0, n).start()

        @pl.when(is_last)
        def _():
            done = jnp.concatenate([x_out[m, k] for k in range(CHUNKS)], axis=1).astype(F32)
            for b in range(SEQ):
                piece = done[8 * b : 8 * b + 8]
                fin_out[m, b] = jnp.concatenate([piece[:, :128], piece[:, 128:]], axis=0).astype(BF16)
            for b in range(SEQ):
                goes_home = jnp.logical_and(is_own_out, i == b)

                @pl.when(goes_home)
                def _():
                    home_copy(m, b).start()

                @pl.when(jnp.logical_not(goes_home))
                def _():
                    fin_copy(m, b).start()

        return carry

    def fin_copy(m, b):
        return pltpu.make_async_remote_copy(
            src_ref=fin_out.at[m, b], dst_ref=fin_in.at[c, m], send_sem=fin_send.at[m, b], recv_sem=fin_recv.at[c, m],
            device_id=(i // PIPE, i % PIPE, b), device_id_type=MESH,
        )

    def home_copy(m, b):
        return pltpu.make_async_copy(fin_out.at[m, b], fin_in.at[c, m], fin_recv.at[c, m])

    lax.fori_loop(0, MICRO, patch_step, 0)

    def drain_pos(k, carry):
        pos_copy(k).wait_send()
        return carry

    lax.fori_loop(1, SEQ, drain_pos, 0)

    def drain(m, carry):
        slot = slot_of(m)
        for k in range(CHUNKS):
            for n, off in enumerate(OTHERS):
                if off in RELAY:
                    block_copy(m, i, k, n, at(off), slot).wait_send()
                else:
                    @pl.when(is_first)
                    def _():
                        block_copy(m, i, k, n, at(off), slot).wait_send()
                block_copy(m, at(off), k, FWD + n, sib, slot).wait_send()
            block_copy(m, i, k, OWN_SIB, sib, slot).wait_send()

            @pl.when(s < PIPE - 1)
            def _():
                for n in range(len(DIRECT)):
                    next_copy(m, k, n).wait_send()

        @pl.when(is_last)
        def _():
            for b in range(SEQ):
                @pl.when(jnp.logical_not(jnp.logical_and(is_own_out, i == b)))
                def _():
                    fin_copy(m, b).wait_send()

        return carry

    lax.fori_loop(0, MICRO, drain, 0)

    guided = []
    for m in range(MICRO):
        for branch in range(2):
            pltpu.make_async_remote_copy(
                src_ref=fin_out.at[m, 0], dst_ref=fin_in.at[branch, m], send_sem=fin_send.at[0, 0],
                recv_sem=fin_recv.at[branch, m], device_id=(c, s, sib), device_id_type=MESH,
            ).wait_recv()
        cond = fin_in[0, m].astype(F32)
        uncond = fin_in[1, m].astype(F32)
        piece = uncond + GUIDANCE * (cond - uncond)
        guided.append(jnp.concatenate([piece[:8], piece[8:]], axis=1))
    guided = jnp.concatenate(guided, axis=0).astype(BF16)
    out_ref[...] = jnp.dot(from_sorted, guided, preferred_element_type=F32).astype(BF16)


def body(hidden, modulation, qkv_weight, stale_cache, patch_of):
    vmem, dma = pltpu.VMEM, pltpu.SemaphoreType.DMA
    hbm = pl.BlockSpec(memory_space=pl.ANY)
    return pl.pallas_call(
        kernel,
        out_shape=jax.ShapeDtypeStruct((32, COLS), BF16),
        in_specs=[hbm, hbm, hbm, hbm, pl.BlockSpec(memory_space=pltpu.VMEM)],
        out_specs=pl.BlockSpec(memory_space=pltpu.VMEM),
        scratch_shapes=[
            vmem((2 * MICRO, SEQ, CHUNKS, ROWS, CW), BF16),
            vmem((SEQ, 3, COLS, COLS), BF16),
            vmem((32, D), BF16),
            vmem((3, D), F32),
            vmem((2, 512, COLS), BF16),
            vmem((32, D), F32),
            vmem((2, 512, COLS), BF16),
            vmem((3, ROWS, COLS), F32),
            vmem((ROWS, 128), F32),
            vmem((ROWS, 128), F32),
            vmem((3, 8, COLS), F32),
            vmem((3, 16, COLS), F32),
            vmem((SEQ, 8, 128), F32),
            vmem((MICRO, CHUNKS, ROWS, CW), BF16),
            vmem((MICRO, SEQ, 16, 128), BF16),
            vmem((2, MICRO, 16, 128), BF16),
            dma((3,)),
            dma((SEQ,)),
            dma((SEQ,)),
            dma((SEQ,)),
            dma((MICRO, N_SEND, CHUNKS)),
            dma((MICRO, SEQ, CHUNKS)),
            dma((MICRO, SEQ)),
            dma((2, MICRO)),
        ],
        compiler_params=pltpu.CompilerParams(
            collective_id=0, has_side_effects=True, vmem_limit_bytes=40 * 2**20
        ),
        cost_estimate=pl.CostEstimate(flops=4 * 10**9, bytes_accessed=8 * 2**20, transcendentals=10**6),
        name="layers",
    )(hidden, modulation, qkv_weight, stale_cache, patch_of.reshape(1, 32))


def solution(mesh):
    placed = (
        P("cfg", "seq", None),
        P("pipe", None, None),
        P("pipe", None, None, "seq"),
        P("cfg", "pipe", None, None, "seq"),
        P("seq"),
    )
    return jax.shard_map(
        body, mesh=mesh, in_specs=placed, out_specs=P("seq", ("cfg", "pipe")), check_vma=False
    )
```

time: 787 us -> 172 us (0.22)
  waiting for transfers between devices: 515 us -> 0 us
  Pallas kernels: 0 us -> 165 us
  blocking collectives: 120 us -> 0 us
  matrix products: 59.4 us -> 0 us
  starting transfers between devices: 37.8 us -> 0 us
  other arithmetic: 17.6 us -> 0 us
  between operations: 15.3 us -> 0.02 us
    all_gather x11 -> x0, waiting for transfers between devices: 429 us -> none  [advance(): projected = project(lax.all_gather(normed, 'seq', axis=0, tiled=True))]
    pallas_call x0 -> x1, Pallas kernels: none -> 165 us  [body(): pl.pallas_call(kernel, out_shape=jax.ShapeDtypeStruct((32, COLS), BF16),...]
    all_to_all x11 -> x0, blocking collectives: 109 us -> none  [advance(): lax.all_to_all(mixed_rows, 'seq', split_axis=0, concat_axis=1, tiled=True)]
    psum x1 -> x0, waiting for transfers between devices: 70.7 us -> none  [from_root(): return lax.psum(jnp.where(mine, shard, jnp.zeros_like(shard)), axis)]
    dot_general x33 -> x0, matrix products: 54.9 us -> none  [the longest x11 45.1 us: project(): jnp.einsum('rd,cdh->crh', piece, weights_local, preferred_element_type=jn...]
    ppermute x12 -> x0, starting transfers between devices: 37.7 us -> none  [the longest x11 35 us: from_behind(): return lax.ppermute(block, axis, route)]
    ppermute x12 -> x0, waiting for transfers between devices: 15.7 us -> none  [the longest x11 14.4 us: from_behind(): return lax.ppermute(block, axis, route)]
    unnamed x1 -> x0, blocking collectives: 10.8 us -> none
  transfers between devices with their start and end apart: 24 -> 0, of which waited for: 24 -> 0; matrix products, arithmetic and copies ran while one was open for 0% -> 0% of each run, Pallas kernels for 0% -> 0%
where the time goes in v1:
time: 172 us
  Pallas kernels  165 us (96%)
  local copies, waits for them, and re-layouts  6.87 us (4%)
    pallas_call x1, Pallas kernels, body(): pl.pallas_call(kernel, out_shape=jax.ShapeDtypeStruct((32, COLS), BF16),...  165 us
    unnamed x10, local copies, waits for them, and re-layouts  6.87 us

profile of v1, /device:TPU:1, one launch (start us, length us, event | category | flops | bytes accessed | tf_op | source)
XLA Modules:
  0.0 171.8 jit_solution(10204398394607219005)
XLA Ops:
  0.0 0.8 copy.6.mod_hbm
  0.8 0.0 copy-start
  0.8 2.8 %copy-done = bf16[1,3,4096,256]{3,2,1,0:T(8,128)(2,1)S(1)} copy-done((bf16[1,3,4096,256]{3,2,1,0:T(8,128)(2,1)S(1)}, bf16[1,3,4096,256]{3,2,1,0:T(8,128)(2,1)}, u32[]{:S(2)}) %copy-start) | copy-done | bytes 6291480
  3.6 0.0 copy-start.1
  3.6 1.0 copy-done.1
  4.7 0.0 copy-start.2
  4.7 0.9 copy-done.2
  5.6 0.0 copy-start.3
  5.6 0.7 copy-done.3
  6.3 165.0 %layers.1 = bf16[32,256]{1,0:T(8,128)(2,1)S(1)} custom-call(bf16[1,32,4096]{2,1,0:T(8,128)(2,1)S(1)} %copy-done.2, f32[1,3,4096]{2,1,0:T(4,128)S(1)} %copy.6.mod_hbm, bf16[1,3,4096,256]{3,2,1,0:T(8,128)(2,1)S(1)} %copy-done, bf16[1,1,2,512,256]{4,3,2,1,0:T(8,128)(2,1)S(1)} %copy-done.1, s32[1,32]{1,0:T(1,128)S(1)} %bitcast.1), custom_call_target="tpu_custom_call" | custom-call | flops 4000000000 | bytes 8388608 | tf_op jit(solution)/shard_map/layers/pallas_call | solution.py:440
  171.2 0.6 copy.8
Async XLA Ops:
  0.8 2.8 %copy-start = (bf16[1,3,4096,256]{3,2,1,0:T(8,128)(2,1)S(1)}, bf16[1,3,4096,256]{3,2,1,0:T(8,128)(2,1)}, u32[]{:S(2)}) copy-start(bf16[1,3,4096,256]{3,2,1,0:T(8,128)(2,1)} %w_hbm.1) | copy-start | bytes 18874372
  3.6 1.0 copy-start.1
  4.7 0.9 copy-start.2
  5.6 0.7 copy-start.3

commit v2 on v1

v2 whole, which is shorter than its diff:
```python
import functools

import jax
import jax.numpy as jnp
from jax import lax
from jax.experimental import pallas as pl
from jax.experimental.pallas import tpu as pltpu
from jax.sharding import PartitionSpec as P

F32 = jnp.float32
BF16 = jnp.bfloat16
MESH = pl.DeviceIdType.MESH

HD = 128
D = 4096
MICRO = 4
ROWS = 128
COLS = 256
SEQ = 16
PIPE = 8
GUIDANCE = 5.0
NORM_EPS = 1e-06

OFFSETS = ((0, 0), (0, 1), (2, 0), (2, 1), (1, 0), (3, 0), (1, 1), (3, 1))
BACK = (0, 1, 2, 3, 5, 4, 7, 6)
CHIPS = 8
GROUPS = ((0, 1), (1, 4), (4, 8))
OWN, DIRECT, RELAY = 0, 1, 2
CHUNKS = 2
CW = COLS // CHUNKS


def kernel(
    hid_hbm, mod_hbm, w_hbm, stale_hbm, patch_ref, out_ref,
    x_buf, w_buf, hid, mod, stale, sorted_rows, kv, acc, sum1, sum2, colsum, shifted,
    pos_buf, x_out, fin_out, fin_in,
    load_sem, w_sem, pos_send, pos_recv, plane_sem, fwd_sem, next_sem, recv_sem, fin_send, fin_recv,
):
    c = lax.axis_index("cfg")
    s = lax.axis_index("pipe")
    i = lax.axis_index("seq")
    core = i % 2
    y = (i // 2) % 2
    x = i // 4
    is_first = s == 0
    is_last = s == PIPE - 1
    relay_flip = jnp.where(is_first, 0, 1)

    def at(n, other=0):
        dx, dy = OFFSETS[n]
        return (((x + dx) % 4) * 2 + (y + dy) % 2) * 2 + (core + other) % 2

    def source(side, n):
        return at(n, side + relay_flip if n >= GROUPS[RELAY][0] else side)

    sib = at(0, 1)
    out_col = c * PIPE + s

    loads = [
        pltpu.make_async_copy(hid_hbm.at[0], hid, load_sem.at[0]),
        pltpu.make_async_copy(mod_hbm, mod, load_sem.at[1]),
        pltpu.make_async_copy(stale_hbm.at[0, 0], stale, load_sem.at[2]),
    ]

    def w_copy(b):
        return pltpu.make_async_copy(
            w_hbm.at[0, :, pl.ds(pl.multiple_of(b * COLS, COLS), COLS), :], w_buf.at[b], w_sem.at[b]
        )

    barrier = pltpu.get_barrier_semaphore()

    def greet(target):
        pl.semaphore_signal(barrier, inc=1, device_id=target, device_id_type=MESH)

    def greet_plane(k, carry):
        greet((c, s, (i + k) % SEQ))
        return carry

    lax.fori_loop(1, SEQ, greet_plane, 0)

    @pl.when(s > 0)
    def _():
        for n in range(GROUPS[RELAY][0]):
            greet((c, s - 1, at(n)))

    for branch in range(2):
        is_self = jnp.logical_and(jnp.logical_and(c == branch, is_last), i == out_col)

        @pl.when(jnp.logical_not(is_self))
        def _():
            greet((branch, PIPE - 1, out_col))

    for load in loads:
        load.start()

    def start_w(b, carry):
        w_copy(b).start()
        return carry

    lax.fori_loop(0, SEQ, start_w, 0)

    patch_row = jnp.broadcast_to(patch_ref[...].astype(F32), (32, 32))
    row32 = lax.broadcasted_iota(jnp.int32, (32, 32), 0)
    col32 = lax.broadcasted_iota(jnp.int32, (32, 32), 1)
    patch_col = jnp.sum(jnp.where(row32 == col32, patch_row, 0.0), axis=1, keepdims=True)
    same = jnp.where(patch_row == patch_col, 1.0, 0.0)
    rank_col = jnp.sum(jnp.where(col32 < row32, same, 0.0), axis=1, keepdims=True)
    rank_row = jnp.sum(jnp.where(row32 < col32, same, 0.0), axis=0, keepdims=True)
    pos_row = patch_row[0:1] * 8.0 + rank_row
    pos_col = patch_col * 8.0 + rank_col
    to_sorted = jnp.where(pos_row == row32.astype(F32), 1.0, 0.0).astype(BF16)
    from_sorted = jnp.where(pos_col == col32.astype(F32), 1.0, 0.0).astype(BF16)
    whole_pos = patch_col * float(ROWS) + rank_col + (i * 8).astype(F32)
    row128 = lax.broadcasted_iota(jnp.int32, (32, 128), 0)
    lane128 = lax.broadcasted_iota(jnp.int32, (32, 128), 1)
    placed = jnp.where(lane128 == row128 + (i % 4) * 32, whole_pos, 0.0)
    pos_buf[i] = jnp.broadcast_to(jnp.sum(placed, axis=0, keepdims=True), (8, 128))

    @pl.when(is_first)
    def _():
        loads[0].wait()
        sorted_rows[...] = jnp.dot(to_sorted, hid[...], preferred_element_type=F32)
        for m in range(MICRO):
            for k in range(CHUNKS):
                pieces = [
                    sorted_rows[8 * m : 8 * m + 8, COLS * j + CW * k : COLS * j + CW * (k + 1)] for j in range(SEQ)
                ]
                x_buf[MICRO + m, 0, k, 0] = jnp.concatenate(pieces, axis=0).astype(BF16)

    @pl.when(s > 0)
    def _():
        loads[0].wait()

    is_own_out = jnp.logical_and(is_last, i == out_col)
    expected = (
        (SEQ - 1)
        + jnp.where(is_last, SEQ, GROUPS[RELAY][0])
        - jnp.where(is_own_out, 1, 0)
    )
    pl.semaphore_wait(barrier, expected)

    def pos_copy(k):
        return pltpu.make_async_remote_copy(
            src_ref=pos_buf.at[i], dst_ref=pos_buf.at[i], send_sem=pos_send.at[k], recv_sem=pos_recv.at[i],
            device_id=(c, s, (i + k) % SEQ), device_id_type=MESH,
        )

    def pos_arrival(b):
        return pltpu.make_async_remote_copy(
            src_ref=pos_buf.at[b], dst_ref=pos_buf.at[b], send_sem=pos_send.at[0], recv_sem=pos_recv.at[b],
            device_id=(c, s, sib), device_id_type=MESH,
        )

    def slot_of(m):
        return m + jnp.where(is_first, MICRO, 0)

    def remote(src, dst, send, recv, target):
        return pltpu.make_async_remote_copy(
            src_ref=src, dst_ref=dst, send_sem=send, recv_sem=recv, device_id=target, device_id_type=MESH
        )

    def region(m, side, k, group):
        low, high = GROUPS[group]
        return x_buf.at[slot_of(m), side, k, pl.ds(low, high - low)]

    def plane_copy(m, k, n, flip):
        slot = slot_of(m)
        return remote(
            x_buf.at[slot, 0, k, 0], x_buf.at[slot, 0, k, BACK[n]],
            plane_sem.at[m], recv_sem.at[m, 0, DIRECT if n < GROUPS[RELAY][0] else RELAY, k], (c, s, at(n, flip)),
        )

    def fwd_copy(m, k, group):
        return remote(
            region(m, 0, k, group), region(m, 1, k, group), fwd_sem.at[m], recv_sem.at[m, 1, group, k], (c, s, sib)
        )

    def next_copy(m, k, n):
        return remote(
            x_out.at[m, k], x_buf.at[m, 0, k, n],
            next_sem.at[m], recv_sem.at[m, 0, OWN if n == 0 else DIRECT, k], (c, s + 1, at(n)),
        )

    def arrive(m, side, k, group):
        here = region(m, side, k, group)
        remote(here, here, fwd_sem.at[m], recv_sem.at[m, side, group, k], (c, s, sib)).wait_recv()

    def take(m, group):
        for k in range(CHUNKS):
            arrive(m, 0, k, group)
            fwd_copy(m, k, group).start()

    def take_sib(m, *groups):
        for group in groups:
            for k in range(CHUNKS):
                arrive(m, 1, k, group)

    def spread_first(m):
        for n in range(1, CHIPS):
            for k in range(CHUNKS):
                plane_copy(m, k, n, 0).start()
        for k in range(CHUNKS):
            fwd_copy(m, k, OWN).start()

    def spread_relay(m):
        for k in range(CHUNKS):
            arrive(m, 0, k, OWN)
            for n in range(*GROUPS[RELAY]):
                plane_copy(m, k, n, 1).start()
            fwd_copy(m, k, OWN).start()

    @pl.when(is_first)
    def _():
        spread_first(0)

    def send_pos(k, carry):
        pos_copy(k).start()
        return carry

    lax.fori_loop(1, SEQ, send_pos, 0)

    loads[1].wait()
    colsum[...] = jnp.zeros_like(colsum)
    shifted[...] = jnp.zeros_like(shifted)

    def fold(b, carry):
        w_copy(b).wait()
        gain = jnp.concatenate(
            [jnp.broadcast_to(1.0 + mod[pl.ds(32 + 2 * b + n, 1), :], (128, 128)).T for n in range(2)], axis=0
        )
        gain = jnp.concatenate([gain, gain], axis=1)
        shift = jnp.broadcast_to(
            jnp.concatenate([mod[pl.ds(2 * b + n, 1), :] for n in range(2)], axis=1), (8, COLS)
        )
        shift_high = shift.astype(BF16)
        shift_low = (shift - shift_high.astype(F32)).astype(BF16)
        shift_both = jnp.concatenate([shift_high, shift_low], axis=0)
        ones = jnp.ones((8, COLS), BF16)
        for t in range(3):
            raw = w_buf[b, t]
            shifted[t] += jnp.dot(shift_both, raw, preferred_element_type=F32)
            scaled = (raw.astype(F32) * gain).astype(BF16)
            w_buf[b, t] = scaled
            colsum[t] += jnp.dot(ones, scaled, preferred_element_type=F32)
        return carry

    lax.fori_loop(0, SEQ // 2, fold, 0)

    @pl.when(is_first)
    def _():
        spread_first(1)

    lax.fori_loop(SEQ // 2, SEQ, fold, 0)

    loads[2].wait()

    def wait_pos(k, carry):
        pos_arrival((i + k) % SEQ).wait_recv()
        return carry

    lax.fori_loop(1, SEQ, wait_pos, 0)
    pos_all = jnp.concatenate(
        [sum(pos_buf[4 * g + n, 0:1, :] for n in range(4)) for g in range(4)], axis=1
    )
    for g in range(4):
        rows = lax.broadcasted_iota(jnp.int32, (128, 512), 0).astype(F32) + float(128 * g)
        pick = jnp.where(pos_all == rows, 1.0, 0.0).astype(BF16)
        for t in range(2):
            kv[t, 128 * g : 128 * g + 128, :] = jnp.dot(
                pick, stale[t], preferred_element_type=F32
            ).astype(BF16)

    @pl.when(s > 0)
    def _():
        spread_relay(0)

    def block(m, side, n):
        return jnp.concatenate([x_buf[m, side, k, n] for k in range(CHUNKS)], axis=1)

    def project(m, side, low, high):
        parts = [block(m, side, n) for n in range(low, high)]
        rows = [source(side, n) for n in range(low, high)]
        fresh = side == 0 and low == 0
        for t in range(3):
            total = sum(jnp.dot(part, w_buf[b, t], preferred_element_type=F32) for part, b in zip(parts, rows))
            acc[t] = total if fresh else acc[t] + total
        one = jnp.zeros((ROWS, 128), F32) if fresh else sum1[...]
        two = jnp.zeros((ROWS, 128), F32) if fresh else sum2[...]
        for part in parts:
            wide = part.astype(F32)
            square = wide * wide
            one = one + wide[:, :128] + wide[:, 128:]
            two = two + square[:, :128] + square[:, 128:]
        sum1[...] = one
        sum2[...] = two

    scaling = 1.0 / (HD ** 0.5)

    def patch_step(m, carry):
        @pl.when(is_first)
        def _():
            take(m, DIRECT)
            take(m, RELAY)
            take_sib(m, OWN, DIRECT, RELAY)

            @pl.when(m < MICRO - 2)
            def _():
                spread_first(m + 2)

            def where_is(b):
                dx = (b // 4 - x + 4) % 4
                dy = ((b // 2) % 2 - y + 2) % 2
                return (b + core) % 2, jnp.where(dx % 2 == 0, dx + dy, 4 + 2 * dy + dx // 2)

            homes = [where_is(b) for b in range(SEQ)]
            for n in range(CHIPS):
                span = pl.ds(pl.multiple_of((at(n) // 2) * 16, 16), 16)
                for k in range(CHUNKS):
                    pieces = [x_buf[MICRO + m, side, k, chip, span, :].astype(F32) for side, chip in homes]
                    for half in range(2):
                        x_buf[m, (half + core) % 2, k, n] = jnp.concatenate(
                            [piece[8 * half : 8 * half + 8] for piece in pieces], axis=0
                        ).astype(BF16)

        @pl.when(s > 0)
        def _():
            take(m, DIRECT)

        project(m, 0, 0, 4)

        @pl.when(s > 0)
        def _():
            take_sib(m, OWN, DIRECT)

        project(m, 1, 0, 4)

        @pl.when(s > 0)
        def _():
            take(m, RELAY)

            @pl.when(m < MICRO - 1)
            def _():
                spread_relay(m + 1)

        project(m, 0, 4, 8)

        @pl.when(s > 0)
        def _():
            take_sib(m, RELAY)

        project(m, 1, 4, 8)

        mean = jnp.sum(sum1[...], axis=1, keepdims=True) * (1.0 / D)
        var = jnp.sum(sum2[...], axis=1, keepdims=True) * (1.0 / D) - mean * mean
        inv = lax.rsqrt(var + NORM_EPS)

        def finish(t):
            bias = shifted[t, 0:1] + shifted[t, 8:9]
            return (inv * (acc[t] - mean * colsum[t, 0:1]) + bias).astype(BF16)

        query = finish(0)
        rows = pl.ds(pl.multiple_of(m * ROWS, ROWS), ROWS)
        kv[0, rows, :] = finish(1)
        kv[1, rows, :] = finish(2)
        old = block(m, 0, 0)
        for h in range(2):
            cols = slice(h * HD, (h + 1) * HD)
            scores = lax.dot_general(
                query[:, cols], kv[0, :, cols], (((1,), (1,)), ((), ())), preferred_element_type=F32
            )
            top = jnp.max(scores, axis=1, keepdims=True)
            weights = jnp.exp((scores - top) * scaling)
            norm = jnp.sum(weights, axis=1, keepdims=True)
            mixed = jnp.dot(weights.astype(BF16), kv[1, :, cols], preferred_element_type=F32) / norm
            mixed = mixed.astype(BF16).astype(F32)
            fresh = (old[:, cols].astype(F32) + mod[pl.ds(64 + 2 * i + h, 1), :] * mixed).astype(BF16)
            x_out[m, h] = fresh

            @pl.when(s < PIPE - 1)
            def _():
                next_copy(m, h, 0).start()
                if h == 1:
                    for k in range(CHUNKS):
                        for n in range(1, GROUPS[RELAY][0]):
                            next_copy(m, k, n).start()

        @pl.when(is_last)
        def _():
            done = jnp.concatenate([x_out[m, k] for k in range(CHUNKS)], axis=1).astype(F32)
            for b in range(SEQ):
                piece = done[8 * b : 8 * b + 8]
                fin_out[m, b] = jnp.concatenate([piece[:, :128], piece[:, 128:]], axis=0).astype(BF16)

            @pl.when(is_own_out)
            def _():
                home_copy(m).start()

                def send(k, inner):
                    fin_copy(m, (i + k) % SEQ).start()
                    return inner

                lax.fori_loop(1, SEQ, send, 0)

            @pl.when(jnp.logical_not(is_own_out))
            def _():
                for b in range(SEQ):
                    fin_copy(m, b).start()

        return carry

    def fin_copy(m, b):
        return remote(
            fin_out.at[m, b], fin_in.at[c, m], fin_send.at[m], fin_recv.at[c, m], (i // PIPE, i % PIPE, b)
        )

    def home_copy(m):
        return pltpu.make_async_copy(fin_out.at[m, i], fin_in.at[c, m], fin_recv.at[c, m])

    lax.fori_loop(0, MICRO, patch_step, 0)

    def left(ref, sem):
        remote(ref, ref, sem, recv_sem.at[0, 0, 0, 0], (c, s, sib)).wait_send()

    def drain_pos(k, carry):
        pos_copy(k).wait_send()
        return carry

    lax.fori_loop(1, SEQ, drain_pos, 0)

    for m in range(MICRO):
        left(x_buf.at[0, 0], fwd_sem.at[m])

        @pl.when(is_first)
        def _():
            left(x_buf.at[0, 0, :, pl.ds(0, 7)], plane_sem.at[m])

        @pl.when(s > 0)
        def _():
            left(x_buf.at[0, 0, 0], plane_sem.at[m])

        @pl.when(s < PIPE - 1)
        def _():
            left(x_buf.at[0, 0, 0], next_sem.at[m])

        @pl.when(jnp.logical_and(is_last, is_own_out))
        def _():
            left(fin_out.at[m, pl.ds(0, SEQ - 1)], fin_send.at[m])

        @pl.when(jnp.logical_and(is_last, jnp.logical_not(is_own_out)))
        def _():
            left(fin_out.at[m], fin_send.at[m])

    guided = []
    for m in range(MICRO):
        for branch in range(2):
            here = fin_in.at[branch, m]
            remote(here, here, fin_send.at[m], fin_recv.at[branch, m], (c, s, sib)).wait_recv()
        cond = fin_in[0, m].astype(F32)
        uncond = fin_in[1, m].astype(F32)
        piece = uncond + GUIDANCE * (cond - uncond)
        guided.append(jnp.concatenate([piece[:8], piece[8:]], axis=1))
    guided = jnp.concatenate(guided, axis=0).astype(BF16)
    out_ref[...] = jnp.dot(from_sorted, guided, preferred_element_type=F32).astype(BF16)


def body(hidden, modulation, qkv_weight, stale_cache, patch_of):
    vmem, dma = pltpu.VMEM, pltpu.SemaphoreType.DMA
    hbm = pl.BlockSpec(memory_space=pl.ANY)
    return pl.pallas_call(
        kernel,
        out_shape=jax.ShapeDtypeStruct((32, COLS), BF16),
        in_specs=[hbm, hbm, hbm, hbm, pl.BlockSpec(memory_space=pltpu.VMEM)],
        out_specs=pl.BlockSpec(memory_space=pltpu.VMEM),
        scratch_shapes=[
            vmem((2 * MICRO, 2, CHUNKS, CHIPS, ROWS, CW), BF16),
            vmem((SEQ, 3, COLS, COLS), BF16),
            vmem((32, D), BF16),
            vmem((96, 128), F32),
            vmem((2, 512, COLS), BF16),
            vmem((32, D), F32),
            vmem((2, 512, COLS), BF16),
            vmem((3, ROWS, COLS), F32),
            vmem((ROWS, 128), F32),
            vmem((ROWS, 128), F32),
            vmem((3, 8, COLS), F32),
            vmem((3, 16, COLS), F32),
            vmem((SEQ, 8, 128), F32),
            vmem((MICRO, CHUNKS, ROWS, CW), BF16),
            vmem((MICRO, SEQ, 16, 128), BF16),
            vmem((2, MICRO, 16, 128), BF16),
            dma((3,)),
            dma((SEQ,)),
            dma((SEQ,)),
            dma((SEQ,)),
            dma((MICRO,)),
            dma((MICRO,)),
            dma((MICRO,)),
            dma((MICRO, 2, 3, CHUNKS)),
            dma((MICRO,)),
            dma((2, MICRO)),
        ],
        compiler_params=pltpu.CompilerParams(
            collective_id=0, has_side_effects=True, vmem_limit_bytes=56 * 2**20
        ),
        cost_estimate=pl.CostEstimate(flops=4 * 10**9, bytes_accessed=8 * 2**20, transcendentals=10**6),
        name="layers",
    )(hidden, modulation.reshape(96, 128), qkv_weight, stale_cache, patch_of.reshape(1, 32))


def solution(mesh):
    placed = (
        P("cfg", "seq", None),
        P("pipe", None, None),
        P("pipe", None, None, "seq"),
        P("cfg", "pipe", None, None, "seq"),
        P("seq"),
    )
    return jax.shard_map(
        body, mesh=mesh, in_specs=placed, out_specs=P("seq", ("cfg", "pipe")), check_vma=False
    )
```

time: 172 us -> 152 us (0.88)
  Pallas kernels: 165 us -> 150 us
  local copies, waits for them, and re-layouts: 6.87 us -> 1.32 us
    pallas_call x1, Pallas kernels: 165 us -> 150 us  [body(): pl.pallas_call(kernel, out_shape=jax.ShapeDtypeStruct((32, COLS), BF16),...]
    unnamed x10 -> x1, local copies, waits for them, and re-layouts: 6.87 us -> 1.32 us
where the time goes in v2:
time: 152 us
  Pallas kernels  150 us (99%)
    pallas_call x1, Pallas kernels, body(): pl.pallas_call(kernel, out_shape=jax.ShapeDtypeStruct((32, COLS), BF16),...  150 us

profile of v2, /device:TPU:1, one launch (start us, length us, event | category | flops | bytes accessed | tf_op | source)
XLA Modules:
  0.0 151.8 jit_solution(9473623490385511010)
XLA Ops:
  0.0 150.4 %layers.1 = bf16[32,256]{1,0:T(8,128)(2,1)} custom-call(bf16[1,32,4096]{2,1,0:T(8,128)(2,1)} %hid_hbm.1, f32[96,128]{1,0:T(8,128)} %bitcast.2, bf16[1,3,4096,256]{3,2,1,0:T(8,128)(2,1)} %w_hbm.1, bf16[1,1,2,512,256]{4,3,2,1,0:T(8,128)(2,1)} %stale_hbm.1, s32[1,32]{1,0:T(1,128)} %bitcast.3), custom_call_target="tpu_custom_call" | custom-call | flops 4000000000 | bytes 8388608 | tf_op jit(solution)/shard_map/layers/pallas_call | solution.py:469
  150.5 1.3 copy.7

commit v3 on v2

--- a/solution.py
+++ b/solution.py
@@ -21,10 +21,11 @@
 GUIDANCE = 5.0
 NORM_EPS = 1e-06
 
-OFFSETS = ((0, 0), (0, 1), (2, 0), (2, 1), (1, 0), (3, 0), (1, 1), (3, 1))
-BACK = (0, 1, 2, 3, 5, 4, 7, 6)
+OFFSETS = ((0, 0), (1, 1), (3, 1), (2, 1), (1, 0), (3, 0), (2, 0), (0, 1))
+BACK = tuple(OFFSETS.index(((4 - dx) % 4, dy)) for dx, dy in OFFSETS)
 CHIPS = 8
-GROUPS = ((0, 1), (1, 4), (4, 8))
+N_DIRECT = 4
+GROUPS = ((0, 1), (1, N_DIRECT), (N_DIRECT, CHIPS))
 OWN, DIRECT, RELAY = 0, 1, 2
 CHUNKS = 2
 CW = COLS // CHUNKS
@@ -51,7 +52,7 @@
         return (((x + dx) % 4) * 2 + (y + dy) % 2) * 2 + (core + other) % 2
 
     def source(side, n):
-        return at(n, side + relay_flip if n >= GROUPS[RELAY][0] else side)
+        return at(n, side + relay_flip if n >= N_DIRECT else side)
 
     sib = at(0, 1)
     out_col = c * PIPE + s
@@ -80,7 +81,7 @@
 
     @pl.when(s > 0)
     def _():
-        for n in range(GROUPS[RELAY][0]):
+        for n in range(N_DIRECT):
             greet((c, s - 1, at(n)))
 
     for branch in range(2):
@@ -96,8 +97,6 @@
     def start_w(b, carry):
         w_copy(b).start()
         return carry
-
-    lax.fori_loop(0, SEQ, start_w, 0)
 
     patch_row = jnp.broadcast_to(patch_ref[...].astype(F32), (32, 32))
     row32 = lax.broadcasted_iota(jnp.int32, (32, 32), 0)
@@ -116,9 +115,11 @@
     placed = jnp.where(lane128 == row128 + (i % 4) * 32, whole_pos, 0.0)
     pos_buf[i] = jnp.broadcast_to(jnp.sum(placed, axis=0, keepdims=True), (8, 128))
 
+    loads[0].wait()
+    lax.fori_loop(0, SEQ, start_w, 0)
+
     @pl.when(is_first)
     def _():
-        loads[0].wait()
         sorted_rows[...] = jnp.dot(to_sorted, hid[...], preferred_element_type=F32)
         for m in range(MICRO):
             for k in range(CHUNKS):
@@ -127,14 +128,10 @@
                 ]
                 x_buf[MICRO + m, 0, k, 0] = jnp.concatenate(pieces, axis=0).astype(BF16)
 
-    @pl.when(s > 0)
-    def _():
-        loads[0].wait()
-
     is_own_out = jnp.logical_and(is_last, i == out_col)
     expected = (
         (SEQ - 1)
-        + jnp.where(is_last, SEQ, GROUPS[RELAY][0])
+        + jnp.where(is_last, SEQ, N_DIRECT)
         - jnp.where(is_own_out, 1, 0)
     )
     pl.semaphore_wait(barrier, expected)
@@ -163,11 +160,12 @@
         low, high = GROUPS[group]
         return x_buf.at[slot_of(m), side, k, pl.ds(low, high - low)]
 
-    def plane_copy(m, k, n, flip):
+    def plane_copy(m, k, n):
         slot = slot_of(m)
+        group = DIRECT if n < N_DIRECT else RELAY
         return remote(
             x_buf.at[slot, 0, k, 0], x_buf.at[slot, 0, k, BACK[n]],
-            plane_sem.at[m], recv_sem.at[m, 0, DIRECT if n < GROUPS[RELAY][0] else RELAY, k], (c, s, at(n, flip)),
+            plane_sem.at[m], recv_sem.at[m, 0, group, k], (c, s, at(n, relay_flip)),
         )
 
     def fwd_copy(m, k, group):
@@ -177,7 +175,7 @@
 
     def next_copy(m, k, n):
         return remote(
-            x_out.at[m, k], x_buf.at[m, 0, k, n],
+            x_out.at[m, k], x_buf.at[m, 0, k, BACK[n]],
             next_sem.at[m], recv_sem.at[m, 0, OWN if n == 0 else DIRECT, k], (c, s + 1, at(n)),
         )
 
@@ -195,23 +193,25 @@
             for k in range(CHUNKS):
                 arrive(m, 1, k, group)
 
+    def spread(m):
+        for k in range(CHUNKS):
+            @pl.when(s > 0)
+            def _():
+                arrive(m, 0, k, OWN)
+
+            for n in range(*GROUPS[RELAY]):
+                plane_copy(m, k, n).start()
+            fwd_copy(m, k, OWN).start()
+
     def spread_first(m):
-        for n in range(1, CHIPS):
+        @pl.when(is_first)
+        def _():
             for k in range(CHUNKS):
-                plane_copy(m, k, n, 0).start()
-        for k in range(CHUNKS):
-            fwd_copy(m, k, OWN).start()
-
-    def spread_relay(m):
-        for k in range(CHUNKS):
-            arrive(m, 0, k, OWN)
-            for n in range(*GROUPS[RELAY]):
-                plane_copy(m, k, n, 1).start()
-            fwd_copy(m, k, OWN).start()
-
-    @pl.when(is_first)
-    def _():
-        spread_first(0)
+                for n in range(*GROUPS[DIRECT]):
+                    plane_copy(m, k, n).start()
+            spread(m)
+
+    spread_first(0)
 
     def send_pos(k, carry):
         pos_copy(k).start()
@@ -246,11 +246,11 @@
 
     lax.fori_loop(0, SEQ // 2, fold, 0)
 
-    @pl.when(is_first)
-    def _():
-        spread_first(1)
+    spread_first(1)
 
     lax.fori_loop(SEQ // 2, SEQ, fold, 0)
+
+    spread_first(2)
 
     loads[2].wait()
 
@@ -270,9 +270,11 @@
                 pick, stale[t], preferred_element_type=F32
             ).astype(BF16)
 
+    spread_first(3)
+
     @pl.when(s > 0)
     def _():
-        spread_relay(0)
+        spread(0)
 
     def block(m, side, n):
         return jnp.concatenate([x_buf[m, side, k, n] for k in range(CHUNKS)], axis=1)
@@ -303,14 +305,11 @@
             take(m, RELAY)
             take_sib(m, OWN, DIRECT, RELAY)
 
-            @pl.when(m < MICRO - 2)
-            def _():
-                spread_first(m + 2)
-
             def where_is(b):
-                dx = (b // 4 - x + 4) % 4
-                dy = ((b // 2) % 2 - y + 2) % 2
-                return (b + core) % 2, jnp.where(dx % 2 == 0, dx + dy, 4 + 2 * dy + dx // 2)
+                chip = 0
+                for n in range(1, CHIPS):
+                    chip = chip + jnp.where(at(n) // 2 == b // 2, n, 0)
+                return (b + core) % 2, chip
 
             homes = [where_is(b) for b in range(SEQ)]
             for n in range(CHIPS):
@@ -326,29 +325,25 @@
         def _():
             take(m, DIRECT)
 
-        project(m, 0, 0, 4)
+        project(m, 0, 0, N_DIRECT)
 
         @pl.when(s > 0)
         def _():
-            take_sib(m, OWN, DIRECT)
-
-        project(m, 1, 0, 4)
-
-        @pl.when(s > 0)
-        def _():
-            take(m, RELAY)
-
             @pl.when(m < MICRO - 1)
             def _():
-                spread_relay(m + 1)
-
-        project(m, 0, 4, 8)
+                spread(m + 1)
+
+            take(m, RELAY)
+            take_sib(m, OWN, DIRECT)
+
+        project(m, 1, 0, N_DIRECT)
+        project(m, 0, N_DIRECT, CHIPS)
 
         @pl.when(s > 0)
         def _():
             take_sib(m, RELAY)
 
-        project(m, 1, 4, 8)
+        project(m, 1, N_DIRECT, CHIPS)
 
         mean = jnp.sum(sum1[...], axis=1, keepdims=True) * (1.0 / D)
         var = jnp.sum(sum2[...], axis=1, keepdims=True) * (1.0 / D) - mean * mean
@@ -381,7 +376,7 @@
                 next_copy(m, h, 0).start()
                 if h == 1:
                     for k in range(CHUNKS):
-                        for n in range(1, GROUPS[RELAY][0]):
+                        for n in range(1, N_DIRECT):
                             next_copy(m, k, n).start()
 
         @pl.when(is_last)
@@ -430,17 +425,18 @@
     for m in range(MICRO):
         left(x_buf.at[0, 0], fwd_sem.at[m])
 
+
         @pl.when(is_first)
         def _():
-            left(x_buf.at[0, 0, :, pl.ds(0, 7)], plane_sem.at[m])
+            left(x_buf.at[0, 0, :, pl.ds(0, CHIPS - 1)], plane_sem.at[m])
 
         @pl.when(s > 0)
         def _():
-            left(x_buf.at[0, 0, 0], plane_sem.at[m])
+            left(x_buf.at[0, 0, :, pl.ds(0, CHIPS - N_DIRECT)], plane_sem.at[m])
 
         @pl.when(s < PIPE - 1)
         def _():
-            left(x_buf.at[0, 0, 0], next_sem.at[m])
+            left(x_buf.at[0, 0, :, pl.ds(0, N_DIRECT)], next_sem.at[m])
 
         @pl.when(jnp.logical_and(is_last, is_own_out))
         def _():

time: 152 us -> 143 us (0.941)
  Pallas kernels: 150 us -> 141 us
    pallas_call x1, Pallas kernels: 150 us -> 141 us  [body(): pl.pallas_call(kernel, out_shape=jax.ShapeDtypeStruct((32, COLS), BF16),...]
where the time goes in v3:
time: 143 us
  Pallas kernels  141 us (99%)
    pallas_call x1, Pallas kernels, body(): pl.pallas_call(kernel, out_shape=jax.ShapeDtypeStruct((32, COLS), BF16),...  141 us

profile of v3, /device:TPU:1, one launch (start us, length us, event | category | flops | bytes accessed | tf_op | source)
XLA Modules:
  0.0 142.6 jit_solution(13435125561036507846)
XLA Ops:
  0.0 141.3 %layers.1 = bf16[32,256]{1,0:T(8,128)(2,1)} custom-call(bf16[1,32,4096]{2,1,0:T(8,128)(2,1)} %hid_hbm.1, f32[96,128]{1,0:T(8,128)} %bitcast.2, bf16[1,3,4096,256]{3,2,1,0:T(8,128)(2,1)} %w_hbm.1, bf16[1,1,2,512,256]{4,3,2,1,0:T(8,128)(2,1)} %stale_hbm.1, s32[1,32]{1,0:T(1,128)} %bitcast.3), custom_call_target="tpu_custom_call" | custom-call | flops 4000000000 | bytes 8388608 | tf_op jit(solution)/shard_map/layers/pallas_call | solution.py:465
  141.3 1.3 copy.7

commit v4 on v3

--- a/solution.py
+++ b/solution.py
@@ -20,6 +20,7 @@
 PIPE = 8
 GUIDANCE = 5.0
 NORM_EPS = 1e-06
+LOG2_E = 1.4426950408889634
 
 OFFSETS = ((0, 0), (1, 1), (3, 1), (2, 1), (1, 0), (3, 0), (2, 0), (0, 1))
 BACK = tuple(OFFSETS.index(((4 - dx) % 4, dy)) for dx, dy in OFFSETS)
@@ -296,7 +297,27 @@
         sum1[...] = one
         sum2[...] = two
 
-    scaling = 1.0 / (HD ** 0.5)
+    def project_half(m, side, k, low, high):
+        pairs = [(n, n + 1) for n in range(low, high, 2)]
+        parts = [jnp.concatenate([x_buf[m, side, k, n] for n in pair], axis=1) for pair in pairs]
+        rows = slice(CW * k, CW * (k + 1))
+        for t in range(3):
+            total = acc[t]
+            for part, pair in zip(parts, pairs):
+                weight = jnp.concatenate([w_buf[source(side, n), t, rows, :] for n in pair], axis=0)
+                total = total + jnp.dot(part, weight, preferred_element_type=F32)
+            acc[t] = total
+        one = sum1[...]
+        two = sum2[...]
+        for part in parts:
+            wide = part.astype(F32)
+            square = wide * wide
+            one = one + wide[:, :128] + wide[:, 128:]
+            two = two + square[:, :128] + square[:, 128:]
+        sum1[...] = one
+        sum2[...] = two
+
+    scaling = LOG2_E / (HD ** 0.5)
 
     def patch_step(m, carry):
         @pl.when(is_first)
@@ -325,25 +346,29 @@
         def _():
             take(m, DIRECT)
 
-        project(m, 0, 0, N_DIRECT)
-
         @pl.when(s > 0)
         def _():
             @pl.when(m < MICRO - 1)
             def _():
                 spread(m + 1)
 
+        project(m, 0, 0, N_DIRECT)
+
+        @pl.when(s > 0)
+        def _():
+
             take(m, RELAY)
             take_sib(m, OWN, DIRECT)
 
         project(m, 1, 0, N_DIRECT)
         project(m, 0, N_DIRECT, CHIPS)
 
-        @pl.when(s > 0)
-        def _():
-            take_sib(m, RELAY)
-
-        project(m, 1, N_DIRECT, CHIPS)
+        for k in range(CHUNKS):
+            @pl.when(s > 0)
+            def _():
+                arrive(m, 1, k, RELAY)
+
+            project_half(m, 1, k, N_DIRECT, CHIPS)
 
         mean = jnp.sum(sum1[...], axis=1, keepdims=True) * (1.0 / D)
         var = jnp.sum(sum2[...], axis=1, keepdims=True) * (1.0 / D) - mean * mean
@@ -364,9 +389,9 @@
                 query[:, cols], kv[0, :, cols], (((1,), (1,)), ((), ())), preferred_element_type=F32
             )
             top = jnp.max(scores, axis=1, keepdims=True)
-            weights = jnp.exp((scores - top) * scaling)
-            norm = jnp.sum(weights, axis=1, keepdims=True)
-            mixed = jnp.dot(weights.astype(BF16), kv[1, :, cols], preferred_element_type=F32) / norm
+            weights = jnp.exp2((scores - top) * scaling)
+            norm = 1.0 / jnp.sum(weights, axis=1, keepdims=True)
+            mixed = jnp.dot(weights.astype(BF16), kv[1, :, cols], preferred_element_type=F32) * norm
             mixed = mixed.astype(BF16).astype(F32)
             fresh = (old[:, cols].astype(F32) + mod[pl.ds(64 + 2 * i + h, 1), :] * mixed).astype(BF16)
             x_out[m, h] = fresh

time: 143 us -> 140 us (0.979)
  Pallas kernels: 141 us -> 139 us
    pallas_call x1, Pallas kernels: 141 us -> 139 us  [body(): pl.pallas_call(kernel, out_shape=jax.ShapeDtypeStruct((32, COLS), BF16),...]
where the time goes in v4:
time: 140 us
  Pallas kernels  139 us (99%)
    pallas_call x1, Pallas kernels, body(): pl.pallas_call(kernel, out_shape=jax.ShapeDtypeStruct((32, COLS), BF16),...  139 us

profile of v4, /device:TPU:1, one launch (start us, length us, event | category | flops | bytes accessed | tf_op | source)
XLA Modules:
  0.0 140.3 jit_solution(8891968766060528575)
XLA Ops:
  0.0 138.9 %layers.1 = bf16[32,256]{1,0:T(8,128)(2,1)} custom-call(bf16[1,32,4096]{2,1,0:T(8,128)(2,1)} %hid_hbm.1, f32[96,128]{1,0:T(8,128)} %bitcast.2, bf16[1,3,4096,256]{3,2,1,0:T(8,128)(2,1)} %w_hbm.1, bf16[1,1,2,512,256]{4,3,2,1,0:T(8,128)(2,1)} %stale_hbm.1, s32[1,32]{1,0:T(1,128)} %bitcast.3), custom_call_target="tpu_custom_call" | custom-call | flops 4000000000 | bytes 8388608 | tf_op jit(solution)/shard_map/layers/pallas_call | solution.py:490
  138.9 1.3 copy.7

commit v5 on v4

--- a/solution.py
+++ b/solution.py
@@ -22,12 +22,13 @@
 NORM_EPS = 1e-06
 LOG2_E = 1.4426950408889634
 
-OFFSETS = ((0, 0), (1, 1), (3, 1), (2, 1), (1, 0), (3, 0), (2, 0), (0, 1))
+OFFSETS = ((0, 0), (1, 1), (3, 1), (2, 1), (0, 1), (1, 0), (3, 0), (2, 0))
 BACK = tuple(OFFSETS.index(((4 - dx) % 4, dy)) for dx, dy in OFFSETS)
 CHIPS = 8
 N_DIRECT = 4
-GROUPS = ((0, 1), (1, N_DIRECT), (N_DIRECT, CHIPS))
-OWN, DIRECT, RELAY = 0, 1, 2
+GROUPS = ((0, 1), (1, N_DIRECT), (N_DIRECT, CHIPS - 1), (CHIPS - 1, CHIPS))
+OWN, DIRECT, RELAY, FAR = 0, 1, 2, 3
+RELAY_ORDER = (5, 6, 7, 4)
 CHUNKS = 2
 CW = COLS // CHUNKS
 
@@ -53,7 +54,7 @@
         return (((x + dx) % 4) * 2 + (y + dy) % 2) * 2 + (core + other) % 2
 
     def source(side, n):
-        return at(n, side + relay_flip if n >= N_DIRECT else side)
+        return at(n, side + relay_flip if n > 0 else side)
 
     sib = at(0, 1)
     out_col = c * PIPE + s
@@ -83,7 +84,7 @@
     @pl.when(s > 0)
     def _():
         for n in range(N_DIRECT):
-            greet((c, s - 1, at(n)))
+            greet((c, s - 1, at(n, 1 if n else 0)))
 
     for branch in range(2):
         is_self = jnp.logical_and(jnp.logical_and(c == branch, is_last), i == out_col)
@@ -163,7 +164,7 @@
 
     def plane_copy(m, k, n):
         slot = slot_of(m)
-        group = DIRECT if n < N_DIRECT else RELAY
+        group = DIRECT if n < N_DIRECT else RELAY if n < CHIPS - 1 else FAR
         return remote(
             x_buf.at[slot, 0, k, 0], x_buf.at[slot, 0, k, BACK[n]],
             plane_sem.at[m], recv_sem.at[m, 0, group, k], (c, s, at(n, relay_flip)),
@@ -177,17 +178,18 @@
     def next_copy(m, k, n):
         return remote(
             x_out.at[m, k], x_buf.at[m, 0, k, BACK[n]],
-            next_sem.at[m], recv_sem.at[m, 0, OWN if n == 0 else DIRECT, k], (c, s + 1, at(n)),
+            next_sem.at[m], recv_sem.at[m, 0, OWN if n == 0 else DIRECT, k], (c, s + 1, at(n, 1 if n else 0)),
         )
 
     def arrive(m, side, k, group):
         here = region(m, side, k, group)
         remote(here, here, fwd_sem.at[m], recv_sem.at[m, side, group, k], (c, s, sib)).wait_recv()
 
-    def take(m, group):
+    def take(m, *groups):
         for k in range(CHUNKS):
-            arrive(m, 0, k, group)
-            fwd_copy(m, k, group).start()
+            for group in groups:
+                arrive(m, 0, k, group)
+                fwd_copy(m, k, group).start()
 
     def take_sib(m, *groups):
         for group in groups:
@@ -200,7 +202,7 @@
             def _():
                 arrive(m, 0, k, OWN)
 
-            for n in range(*GROUPS[RELAY]):
+            for n in RELAY_ORDER:
                 plane_copy(m, k, n).start()
             fwd_copy(m, k, OWN).start()
 
@@ -322,9 +324,8 @@
     def patch_step(m, carry):
         @pl.when(is_first)
         def _():
-            take(m, DIRECT)
-            take(m, RELAY)
-            take_sib(m, OWN, DIRECT, RELAY)
+            take(m, DIRECT, RELAY, FAR)
+            take_sib(m, OWN, DIRECT, RELAY, FAR)
 
             def where_is(b):
                 chip = 0
@@ -344,29 +345,26 @@
 
         @pl.when(s > 0)
         def _():
-            take(m, DIRECT)
-
-        @pl.when(s > 0)
-        def _():
             @pl.when(m < MICRO - 1)
             def _():
                 spread(m + 1)
 
+            take(m, DIRECT, RELAY, FAR)
+
         project(m, 0, 0, N_DIRECT)
+        project(m, 0, N_DIRECT, CHIPS)
 
         @pl.when(s > 0)
         def _():
-
-            take(m, RELAY)
             take_sib(m, OWN, DIRECT)
 
         project(m, 1, 0, N_DIRECT)
-        project(m, 0, N_DIRECT, CHIPS)
 
         for k in range(CHUNKS):
             @pl.when(s > 0)
             def _():
                 arrive(m, 1, k, RELAY)
+                arrive(m, 1, k, FAR)
 
             project_half(m, 1, k, N_DIRECT, CHIPS)
 
@@ -516,7 +514,7 @@
             dma((MICRO,)),
             dma((MICRO,)),
             dma((MICRO,)),
-            dma((MICRO, 2, 3, CHUNKS)),
+            dma((MICRO, 2, 4, CHUNKS)),
             dma((MICRO,)),
             dma((2, MICRO)),
         ],

time: 140 us -> 137 us (0.979)
  Pallas kernels: 139 us -> 136 us
    pallas_call x1, Pallas kernels: 139 us -> 136 us  [body(): pl.pallas_call(kernel, out_shape=jax.ShapeDtypeStruct((32, COLS), BF16),...]
where the time goes in v5:
time: 137 us
  Pallas kernels  136 us (99%)
    pallas_call x1, Pallas kernels, body(): pl.pallas_call(kernel, out_shape=jax.ShapeDtypeStruct((32, COLS), BF16),...  136 us

profile of v5, /device:TPU:1, one launch (start us, length us, event | category | flops | bytes accessed | tf_op | source)
XLA Modules:
  0.0 137.3 jit_solution(16286766770350192768)
XLA Ops:
  0.0 136.0 %layers.1 = bf16[32,256]{1,0:T(8,128)(2,1)} custom-call(bf16[1,32,4096]{2,1,0:T(8,128)(2,1)} %hid_hbm.1, f32[96,128]{1,0:T(8,128)} %bitcast.2, bf16[1,3,4096,256]{3,2,1,0:T(8,128)(2,1)} %w_hbm.1, bf16[1,1,2,512,256]{4,3,2,1,0:T(8,128)(2,1)} %stale_hbm.1, s32[1,32]{1,0:T(1,128)} %bitcast.3), custom_call_target="tpu_custom_call" | custom-call | flops 4000000000 | bytes 8388608 | tf_op jit(solution)/shard_map/layers/pallas_call | solution.py:488
  136.0 1.3 copy.7

commit v6 on v5

--- a/solution.py
+++ b/solution.py
@@ -26,9 +26,9 @@
 BACK = tuple(OFFSETS.index(((4 - dx) % 4, dy)) for dx, dy in OFFSETS)
 CHIPS = 8
 N_DIRECT = 4
-GROUPS = ((0, 1), (1, N_DIRECT), (N_DIRECT, CHIPS - 1), (CHIPS - 1, CHIPS))
+GROUPS = ((0, 1), (1, N_DIRECT), (N_DIRECT, CHIPS - 2), (CHIPS - 2, CHIPS))
 OWN, DIRECT, RELAY, FAR = 0, 1, 2, 3
-RELAY_ORDER = (5, 6, 7, 4)
+RELAY_ORDER = (7, 5, 6, 4)
 CHUNKS = 2
 CW = COLS // CHUNKS
 
@@ -164,9 +164,10 @@
 
     def plane_copy(m, k, n):
         slot = slot_of(m)
-        group = DIRECT if n < N_DIRECT else RELAY if n < CHIPS - 1 else FAR
+        there = BACK[n]
+        group = DIRECT if there < N_DIRECT else RELAY if there < CHIPS - 2 else FAR
         return remote(
-            x_buf.at[slot, 0, k, 0], x_buf.at[slot, 0, k, BACK[n]],
+            x_buf.at[slot, 0, k, 0], x_buf.at[slot, 0, k, there],
             plane_sem.at[m], recv_sem.at[m, 0, group, k], (c, s, at(n, relay_flip)),
         )
 

time: 137 us -> 136 us (level)
    pallas_call x1, Pallas kernels: 136 us -> 135 us  [body(): pl.pallas_call(kernel, out_shape=jax.ShapeDtypeStruct((32, COLS), BF16),...]
where the time goes in v6:
time: 136 us
  Pallas kernels  135 us (99%)
    pallas_call x1, Pallas kernels, body(): pl.pallas_call(kernel, out_shape=jax.ShapeDtypeStruct((32, COLS), BF16),...  135 us

profile of v6, /device:TPU:1, one launch (start us, length us, event | category | flops | bytes accessed | tf_op | source)
XLA Modules:
  0.0 135.9 jit_solution(13682596842031494037)
XLA Ops:
  0.0 134.6 %layers.1 = bf16[32,256]{1,0:T(8,128)(2,1)} custom-call(bf16[1,32,4096]{2,1,0:T(8,128)(2,1)} %hid_hbm.1, f32[96,128]{1,0:T(8,128)} %bitcast.2, bf16[1,3,4096,256]{3,2,1,0:T(8,128)(2,1)} %w_hbm.1, bf16[1,1,2,512,256]{4,3,2,1,0:T(8,128)(2,1)} %stale_hbm.1, s32[1,32]{1,0:T(1,128)} %bitcast.3), custom_call_target="tpu_custom_call" | custom-call | flops 4000000000 | bytes 8388608 | tf_op jit(solution)/shard_map/layers/pallas_call | solution.py:489
  134.6 1.3 copy.7

commit v7 on v6

--- a/solution.py
+++ b/solution.py
@@ -205,6 +205,7 @@
 
             for n in RELAY_ORDER:
                 plane_copy(m, k, n).start()
+        for k in range(CHUNKS):
             fwd_copy(m, k, OWN).start()
 
     def spread_first(m):

time: 136 us -> 135 us (level)
  no operation moved by 1% of the time
where the time goes in v7:
time: 135 us
  Pallas kernels  134 us (99%)
    pallas_call x1, Pallas kernels, body(): pl.pallas_call(kernel, out_shape=jax.ShapeDtypeStruct((32, COLS), BF16),...  134 us

profile of v7, /device:TPU:1, one launch (start us, length us, event | category | flops | bytes accessed | tf_op | source)
XLA Modules:
  0.0 135.2 jit_solution(10790631452979123068)
XLA Ops:
  0.0 133.8 %layers.1 = bf16[32,256]{1,0:T(8,128)(2,1)} custom-call(bf16[1,32,4096]{2,1,0:T(8,128)(2,1)} %hid_hbm.1, f32[96,128]{1,0:T(8,128)} %bitcast.2, bf16[1,3,4096,256]{3,2,1,0:T(8,128)(2,1)} %w_hbm.1, bf16[1,1,2,512,256]{4,3,2,1,0:T(8,128)(2,1)} %stale_hbm.1, s32[1,32]{1,0:T(1,128)} %bitcast.3), custom_call_target="tpu_custom_call" | custom-call | flops 4000000000 | bytes 8388608 | tf_op jit(solution)/shard_map/layers/pallas_call | solution.py:490
  133.9 1.3 copy.7
